TPU v7x, 256 devices: a whole 4x4x8 slice. The times are simulated.
256 devices in a mesh: dp: 4 (over x), context: 16 (over z, core), tensor: 4 (over y).
Axes of the slice: x: 4, y: 4, z: 8, core: 2. Of those that a mesh axis runs over, the one named last changes fastest.
Arguments:
- acceptance_vectors: bfloat16 [8192, 4096], P(('dp', 'context'), 'tensor'), may hold values from -6 to 6
- lookup_vectors: bfloat16 [8192, 4096], P(('dp', 'context'), 'tensor'), may hold values from -6 to 6
- payload_vectors: bfloat16 [8192, 4096], P(('dp', 'context'), 'tensor'), may hold values from -6 to 6
- incontext_adaptation: bfloat16 [8192, 4096], P(('dp', 'context'), 'tensor'), may hold values from 0 to 1
- fading_codes: int32 [4, 2048, 64], P('dp', 'context', 'tensor'), may hold values from 1 to 12288
- stacked_line_pointer: int32 [4, 2048], P('dp', 'context'), may hold values from 0 to 8191, as said below
- article_extents: int32 [4, 4], P('dp'), may hold values from 1 to 1024, 2048 in all within a row
- feature_fading: float32 [4096], P('tensor'), may hold values from 3.90625e-05 to 0.03
- erasure_lookup_scaling: float32 [4096], P('tensor'), may hold values from 0.3 to 3
- lookup_mixture_share: float32 [4096], P('tensor'), may hold values from 0 to 1
- reward_coefficients: float32 [4096], P('tensor'), may hold values from -4 to 4
- cluster_standard_scaling: float32 [4096], P('tensor'), may hold values from 0.1 to 1.9
- cluster_standard_offset: float32 [4096], P('tensor'), may hold values from -3 to 3
- final_projection: bfloat16 [4096, 4096], P('tensor'), may hold values from -0.09375 to 0.09375
Outputs:
- summed: bfloat16 [4, 2048, 4096], P('dp', ('context', 'tensor'))
Inputs may be any that keep to these rules, and one draw needn't show every extreme that they name: `stacked_line_pointer`: A permutation of 0 to 8191. Each packed shard is 128 consecutive packed rows; its rows fall into consecutive groups of 2, and group g of every shard holds only positions g * 128 to (g + 1) * 128 - 1 of the sequences laid end to end. `article_extents`: each sequence's 4 lengths sum to 2048.
All inputs are finite; a program needn't handle non-finite values.
Results may differ from a plain program's by a relative error of at most 0.019.
Values may be sent and summed in bfloat16 or wider, within the bound.
A program may use at most 128 MiB of HBM per device.

v0:
```python
import functools

import jax
import jax.numpy as jnp
from jax import lax
from jax.experimental import pallas as pl
from jax.experimental.pallas import tpu as pltpu
from jax.sharding import PartitionSpec as P

MESH = pl.DeviceIdType.MESH
SPAN = 64
CHUNK = 64
GROUP = 8
SMALL = 8
decay_cap = 0.606531
unit_eps = 1e-06
group_eps = 0.00064
f32 = jnp.float32
bf16 = jnp.bfloat16


def nn(a, b):
    return lax.dot_general(
        a.astype(bf16), b.astype(bf16), (((1,), (0,)), ((), ())), preferred_element_type=f32
    )


def nt(a, b):
    return lax.dot_general(
        a.astype(bf16), b.astype(bf16), (((1,), (1,)), ((), ())), preferred_element_type=f32
    )


def tn(a, b):
    return lax.dot_general(
        a.astype(bf16), b.astype(bf16), (((0,), (0,)), ((), ())), preferred_element_type=f32
    )


def exchange(
    n_ctx,
    n_peers,
    per_seq,
    r_ref,
    k_ref,
    v_ref,
    a_ref,
    code_ref,
    ptr_ref,
    rows_ref,
    meta_ref,
    packed,
    notes,
    send_sem,
    recv_sem,
    note_send,
    note_recv,
    own_sem,
):
    dp = lax.axis_index("dp")
    ctx = lax.axis_index("context")
    me = dp * n_ctx + ctx
    tensor = lax.axis_index("tensor")

    def place(index):
        return (index // n_ctx, lax.rem(index, n_ctx), tensor)

    barrier = pltpu.get_barrier_semaphore()

    def greet(step, carry):
        other = lax.rem(me + step, n_peers)
        pl.semaphore_signal(barrier, inc=1, device_id=place(other), device_id_type=MESH)
        return carry

    lax.fori_loop(1, n_peers, greet, 0)

    tokens = r_ref.shape[0]
    n_dp = n_peers // n_ctx
    for pair in range(n_ctx // 2):
        lanes = slice(128 * pair, 128 * pair + 128)
        left, right = slice(0, SPAN), slice(SPAN, 128)
        r, k, v, a = r_ref[:, lanes], k_ref[:, lanes], v_ref[:, lanes], a_ref[:, lanes]
        for half, part in ((0, left), (1, right)):
            rk = jnp.concatenate([r[:, part], k[:, part]], axis=1)
            va = jnp.concatenate([v[:, part], a[:, part]], axis=1)
            for s in range(n_dp):
                slot = s * n_ctx + 2 * pair + half
                packed[slot, :, 0:128] = rk[s * per_seq : (s + 1) * per_seq]
                packed[slot, :, 128:256] = va[s * per_seq : (s + 1) * per_seq]

    eye = (
        lax.broadcasted_iota(jnp.int32, (tokens, tokens), 0)
        == lax.broadcasted_iota(jnp.int32, (tokens, tokens), 1)
    ).astype(f32)
    codes = lax.dot_general(
        code_ref[...].astype(f32),
        eye,
        (((0,), (0,)), ((), ())),
        precision=lax.Precision.HIGHEST,
        preferred_element_type=f32,
    )
    pointers = ptr_ref[...].astype(f32)
    for c in range(n_ctx):
        notes[c, 0:1, :] = pointers
        notes[c, 1:2, :] = codes[c : c + 1, :]
        notes[c, 2:8, :] = jnp.zeros((6, tokens), f32)

    pl.semaphore_wait(barrier, n_peers - 1)

    own_rows = pltpu.make_async_copy(packed.at[me], rows_ref.at[me], own_sem.at[0])
    own_rows.start()
    own_note = pltpu.make_async_copy(notes.at[ctx], meta_ref.at[ctx], own_sem.at[1])
    own_note.start()

    def note_copy(step):
        other = lax.rem(ctx + step, n_ctx)
        return pltpu.make_async_remote_copy(
            src_ref=notes.at[other],
            dst_ref=meta_ref.at[ctx],
            send_sem=note_send,
            recv_sem=note_recv,
            device_id=(dp, other, tensor),
            device_id_type=MESH,
        )

    def rows_copy(step):
        other = lax.rem(me + step, n_peers)
        return pltpu.make_async_remote_copy(
            src_ref=packed.at[other],
            dst_ref=rows_ref.at[me],
            send_sem=send_sem,
            recv_sem=recv_sem,
            device_id=place(other),
            device_id_type=MESH,
        )

    def send_note(step, carry):
        note_copy(step).start()
        return carry

    def send_rows(step, carry):
        rows_copy(step).start()
        return carry

    lax.fori_loop(1, n_ctx, send_note, 0)
    lax.fori_loop(1, n_peers, send_rows, 0)
    own_rows.wait()
    own_note.wait()
    rest_rows = rows_ref.at[pl.ds(0, n_peers - 1)]
    rest_notes = meta_ref.at[pl.ds(0, n_ctx - 1)]
    pltpu.make_async_copy(rest_notes, rest_notes, note_send).wait()
    pltpu.make_async_copy(rest_notes, rest_notes, note_recv).wait()
    pltpu.make_async_copy(rest_rows, rest_rows, send_sem).wait()
    pltpu.make_async_copy(rest_rows, rest_rows, recv_sem).wait()


def recur(
    n_ctx,
    seq_len,
    rows_ref,
    meta_ref,
    lens_ref,
    rate_ref,
    gain_ref,
    mix_ref,
    bonus_ref,
    scale_ref,
    shift_ref,
    out_ref,
    trans,
    push,
    keep,
    carry_out,
    local_out,
    values,
    state,
):
    ctx = lax.axis_index("context")
    odd = lax.rem(ctx, 2) == 1

    def head_row(ref):
        line = ref[pl.ds(ctx // 2, 1), :]
        return jnp.where(odd, line[:, SPAN:], line[:, :SPAN])

    rate, gain, mix = head_row(rate_ref), head_row(gain_ref), head_row(mix_ref)
    bonus, scale, shift = head_row(bonus_ref), head_row(scale_ref), head_row(shift_ref)
    first = lens_ref[0, 0]
    second = first + lens_ref[0, 1]
    third = second + lens_ref[0, 2]

    def doc_of(position):
        return (
            (position >= first).astype(jnp.int32)
            + (position >= second).astype(jnp.int32)
            + (position >= third).astype(jnp.int32)
        )

    n_src = rows_ref.shape[0]
    block = meta_ref.shape[2]
    half = rows_ref.shape[1] // 2
    notes = meta_ref[...].reshape(n_ctx * 8, block).T
    row_i = lax.broadcasted_iota(jnp.int32, (CHUNK, CHUNK), 0)
    col_i = lax.broadcasted_iota(jnp.int32, (CHUNK, CHUNK), 1)
    tri = (row_i >= col_i).astype(bf16)
    tri3 = jnp.concatenate([tri, tri, tri], axis=1)
    eye = (row_i == col_i).astype(f32)
    within = {}
    size = SMALL
    while size <= CHUNK:
        within[size] = (row_i // size) == (col_i // size)
        size *= 2
    blocks_per_group = GROUP * CHUNK // block

    for group in range(seq_len // (GROUP * CHUNK)):
        base = group * GROUP * CHUNK
        span = GROUP * CHUNK
        phase = group * blocks_per_group // (n_ctx // 2)
        source = rows_ref[:, phase * half : (phase + 1) * half, :].reshape(n_src * half, 4 * SPAN)
        taken, codes = [], []
        for b in range(blocks_per_group):
            c = group * blocks_per_group + b
            pointer = notes[:, c * 8 : c * 8 + 1].astype(jnp.int32)
            where = (pointer // 128) * half + lax.rem(pointer, half)
            pick = (
                lax.broadcasted_iota(jnp.int32, (block, n_src * half), 1) == where
            ).astype(bf16)
            taken.append(nn(pick, source))
            codes.append(notes[:, c * 8 + 1 : c * 8 + 2])
        taken = jnp.concatenate(taken, axis=0)
        code = jnp.concatenate(codes, axis=0)
        r, k = taken[:, :SPAN], taken[:, SPAN : 2 * SPAN]
        v, a = taken[:, 2 * SPAN : 3 * SPAN], taken[:, 3 * SPAN :]
        position = base + lax.broadcasted_iota(jnp.int32, (span, 1), 0)
        doc = doc_of(position)
        starts = doc != doc_of(position - 1)
        before = doc_of(position - lax.rem(position, CHUNK) - 1)
        last = doc_of(position - lax.rem(position, CHUNK) + (CHUNK - 1))
        scaled = k * gain
        unit = scaled * lax.rsqrt(jnp.sum(scaled * scaled, axis=1, keepdims=True) + unit_eps)
        mixed = k * (1.0 + (a - 1.0) * mix)
        erase = jnp.where(starts, 0.0, unit * a)
        extra = jnp.sum(r * mixed * bonus, axis=1, keepdims=True) * v
        decay = -decay_cap * (1.0 - jnp.exp(-rate * code))
        d0 = decay.astype(bf16)
        rest = decay - d0.astype(f32)
        d1 = rest.astype(bf16)
        d2 = (rest - d1.astype(f32)).astype(bf16)
        cums, lasts = [], []
        for j in range(GROUP):
            s = slice(j * CHUNK, (j + 1) * CHUNK)
            cum = nn(tri3, jnp.concatenate([d0[s], d1[s], d2[s]], axis=0))
            cums.append(cum)
            lasts.append(jnp.broadcast_to(cum[CHUNK - 1 :], (CHUNK, SPAN)))
        cum = jnp.concatenate(cums, axis=0)
        end = jnp.concatenate(lasts, axis=0)
        up = jnp.exp(cum)
        down = jnp.exp(-cum)
        unit_up = unit * jnp.exp(cum - decay)
        recept_up = r * up
        erase_down = erase * down
        mixed_down = mixed * down
        alive = doc == before
        unit_start = jnp.where(alive, unit_up, 0.0)
        recept_start = jnp.where(alive, recept_up, 0.0)
        tail = jnp.where(doc == last, jnp.exp(end - cum), 0.0)
        erase_tail = erase * tail
        mixed_tail = mixed * tail
        for j in range(GROUP):
            s = slice(j * CHUNK, (j + 1) * CHUNK)
            chunk = group * GROUP + j
            doc_row = doc_of(
                base + j * CHUNK + lax.broadcasted_iota(jnp.int32, (1, CHUNK), 1)
            )
            same = doc[s] == doc_row
            strict = same & (row_i > col_i)
            inclusive = same & (row_i >= col_i)
            scores = nt(
                jnp.concatenate([unit_up[s], recept_up[s]], axis=0),
                jnp.concatenate([erase_down[s], mixed_down[s]], axis=0),
            )
            erase_mat = jnp.where(strict, scores[:CHUNK, :CHUNK], 0.0)
            write_mat = jnp.where(strict, scores[:CHUNK, CHUNK:], 0.0)
            read_erase = jnp.where(inclusive, scores[CHUNK:, :CHUNK], 0.0)
            read_write = jnp.where(inclusive, scores[CHUNK:, CHUNK:], 0.0)
            power = jnp.where(within[SMALL], -erase_mat, 0.0)
            inverse = eye + power
            size = 2
            while size < SMALL:
                power = nn(power, power)
                inverse = inverse + nn(inverse, power)
                size *= 2
            size = SMALL
            while size < CHUNK:
                off = jnp.where(within[2 * size] & ~within[size], erase_mat, 0.0)
                inverse = inverse - nn(inverse, nn(off, inverse))
                size *= 2
            value = v[s]
            both = nn(jnp.concatenate([write_mat, read_write], axis=0), value)
            solved = nn(inverse, jnp.concatenate([both[:CHUNK], unit_start[s]], axis=1))
            read = nn(read_erase, solved)
            local_out[chunk] = both[CHUNK:] - read[:, :SPAN] + extra[s]
            carry_out[chunk] = (recept_start[s] - read[:, SPAN:]).astype(bf16)
            moved = tn(solved, erase_tail[s])
            trans[chunk] = moved[SPAN:].astype(bf16)
            push[chunk] = tn(value, mixed_tail[s]) - moved[:SPAN]
            ends = jnp.exp(cums[j][CHUNK - 1 :])
            alive_end = doc_of(base + j * CHUNK + CHUNK - 1) == doc_of(base + j * CHUNK - 1)
            keep[chunk] = jnp.broadcast_to(jnp.where(alive_end, ends, 0.0), (8, SPAN))

    n_chunks = seq_len // CHUNK

    def advance(chunk, now):
        state[chunk] = now.astype(bf16)
        return now * keep[chunk][0:1] - nn(now, trans[chunk]) + push[chunk]

    lax.fori_loop(0, n_chunks, advance, jnp.zeros((SPAN, SPAN), f32))

    def finish(index, carry):
        lines = []
        for j in range(2):
            chunk = index * 2 + j
            whole = nt(carry_out[chunk], state[chunk]) + local_out[chunk]
            center = whole - jnp.mean(whole, axis=1, keepdims=True)
            spread = jnp.mean(center * center, axis=1, keepdims=True)
            lines.append(center * lax.rsqrt(spread + group_eps) * scale + shift)
        out_ref[index] = jnp.concatenate(lines, axis=1).astype(bf16)
        return carry

    lax.fori_loop(0, n_chunks // 2, finish, 0)


def vmem():
    return pl.BlockSpec(memory_space=pltpu.VMEM)


def run_recur(n_ctx, seq_len, block, rows, meta, lens, vectors):
    n_chunks = seq_len // CHUNK
    return pl.pallas_call(
        functools.partial(recur, n_ctx, seq_len),
        out_shape=jax.ShapeDtypeStruct((n_ctx, block // 2, 2 * SPAN), bf16),
        in_specs=[vmem(), vmem(), pl.BlockSpec(memory_space=pltpu.SMEM)] + [vmem()] * 6,
        out_specs=vmem(),
        scratch_shapes=[
            pltpu.VMEM((n_chunks, SPAN, SPAN), bf16),
            pltpu.VMEM((n_chunks, SPAN, SPAN), f32),
            pltpu.VMEM((n_chunks, 8, SPAN), f32),
            pltpu.VMEM((n_chunks, CHUNK, SPAN), bf16),
            pltpu.VMEM((n_chunks, CHUNK, SPAN), f32),
            pltpu.VMEM((8, 128), f32),
            pltpu.VMEM((n_chunks, SPAN, SPAN), bf16),
        ],
        compiler_params=pltpu.CompilerParams(vmem_limit_bytes=48 << 20),
    )(rows, meta, lens, *vectors)


def local(
    acceptance_vectors,
    lookup_vectors,
    payload_vectors,
    incontext_adaptation,
    fading_codes,
    stacked_line_pointer,
    article_extents,
    feature_fading,
    erasure_lookup_scaling,
    lookup_mixture_share,
    reward_coefficients,
    cluster_standard_scaling,
    cluster_standard_offset,
    final_projection,
):
    tokens, features = acceptance_vectors.shape
    n_dp = lax.axis_size("dp")
    n_ctx = lax.axis_size("context")
    n_peers = n_dp * n_ctx
    per_seq = tokens // n_dp
    seq_len = tokens * n_ctx
    rows, meta = pl.pallas_call(
        functools.partial(exchange, n_ctx, n_peers, per_seq),
        out_shape=(
            jax.ShapeDtypeStruct((n_peers, per_seq, 4 * SPAN), bf16),
            jax.ShapeDtypeStruct((n_ctx, 8, tokens), f32),
        ),
        in_specs=[vmem()] * 6,
        out_specs=(vmem(), vmem()),
        scratch_shapes=[
            pltpu.VMEM((n_peers, per_seq, 4 * SPAN), bf16),
            pltpu.VMEM((n_ctx, 8, tokens), f32),
            pltpu.SemaphoreType.DMA,
            pltpu.SemaphoreType.DMA,
            pltpu.SemaphoreType.DMA,
            pltpu.SemaphoreType.DMA,
            pltpu.SemaphoreType.DMA((2,)),
        ],
        compiler_params=pltpu.CompilerParams(
            collective_id=0, has_side_effects=True, vmem_limit_bytes=32 << 20
        ),
    )(
        acceptance_vectors,
        lookup_vectors,
        payload_vectors,
        incontext_adaptation,
        fading_codes[0],
        stacked_line_pointer,
    )
    vectors = [
        item.reshape(features // 128, 128)
        for item in (
            feature_fading,
            erasure_lookup_scaling,
            lookup_mixture_share,
            reward_coefficients,
            cluster_standard_scaling,
            cluster_standard_offset,
        )
    ]
    normed = run_recur(n_ctx, seq_len, tokens, rows, meta, article_extents, vectors)
    heads = lax.all_to_all(normed, "context", split_axis=0, concat_axis=0, tiled=True)
    lines = (
        heads.reshape(n_ctx, tokens // 2, 2, SPAN).transpose(2, 1, 0, 3).reshape(tokens, features)
    )
    summed = lax.psum_scatter(
        jnp.dot(lines, final_projection, preferred_element_type=f32).astype(bf16),
        "tensor",
        scatter_dimension=0,
        tiled=True,
    )
    return summed.reshape(1, tokens // lax.axis_size("tensor"), final_projection.shape[1])


def solution(mesh):
    return jax.shard_map(
        local,
        mesh=mesh,
        in_specs=(
            P(("dp", "context"), "tensor"),
            P(("dp", "context"), "tensor"),
            P(("dp", "context"), "tensor"),
            P(("dp", "context"), "tensor"),
            P("dp", "context", "tensor"),
            P("dp", "context"),
            P("dp", None),
            P("tensor"),
            P("tensor"),
            P("tensor"),
            P("tensor"),
            P("tensor"),
            P("tensor"),
            P("tensor", None),
        ),
        out_specs=P("dp", ("context", "tensor"), None),
        check_vma=False,
    )
```

profile of v0, /device:TPU:192, one launch (start us, length us, event | category | flops | bytes accessed | tf_op | source)
XLA Modules:
  0.0 164.2 jit_solution(15172814787583301114)
XLA Ops:
  6.5 0.0 reduce-scatter.2.cloned.1.call-start
  6.5 0.8 copy.16
  7.3 0.0 copy-start
  7.3 0.9 copy-done
  8.3 0.0 copy-start.1
  8.3 0.9 copy-done.1
  9.2 0.0 copy-start.2
  9.2 0.9 copy-done.2
  10.2 0.0 copy-start.3
  10.2 0.9 copy-done.3
  11.1 0.0 copy-start.11
  11.1 0.7 copy-done.11
  11.8 33.4 %shard_map.136 = (bf16[64,32,256]{2,1,0:T(8,128)(2,1)S(1)}, f32[16,8,128]{2,1,0:T(8,128)S(1)}) custom-call(bf16[128,1024]{1,0:T(8,128)(2,1)S(1)} %copy-done, bf16[128,1024]{1,0:T(8,128)(2,1)S(1)} %copy-done.1, bf16[128,1024]{1,0:T(8,128)(2,1)S(1)} %copy-done.2, bf16[128,1024]{1,0:T(8,128)(2,1)S(1)} %copy-done.3, s32[128,16]{1,0:T(8,128)S(1)} %bitcast.15, ...), custom_call_target="tpu_custom_call" | custom-call | tf_op jit(solution)/shard_map/pallas_call | solution.py:378
  45.2 0.0 copy-start.4
  45.2 0.7 copy-done.4
  45.9 0.0 copy-start.5
  45.9 0.7 copy-done.5
  46.6 0.0 copy-start.6
  46.6 0.7 copy-done.6
  47.3 0.0 copy-start.7
  47.3 0.7 copy-done.7
  47.9 0.7 copy-done.8
  48.6 0.7 copy-done.9
  49.3 0.7 copy-done.10
  50.0 60.7 %shard_map.137 = bf16[16,64,128]{2,1,0:T(8,128)(2,1)S(1)} custom-call(bf16[64,32,256]{2,1,0:T(8,128)(2,1)S(1)} %get-tuple-element.7.rows_ref, f32[16,8,128]{2,1,0:T(8,128)S(1)} %get-tuple-element.8.meta_ref, s32[1,4]{1,0:T(1,128)S(1)} %copy-done.10, f32[8,128]{1,0:T(8,128)S(1)} %bitcast.16, f32[8,128]{1,0:T(8,128)S(1)} %bitcast.17, f32[8,128]{1,0:T(8,128)S(1)} %bitcast.18, ...), custom_call_target="tpu_custom_call" | custom-call | tf_op jit(solution)/shard_map/pallas_call | solution.py:338
  110.6 13.8 %all_to_all.5 = bf16[16,64,128]{2,1,0:T(8,128)(2,1)S(1)} all-to-all(bf16[16,64,128]{2,1,0:T(8,128)(2,1)S(1)} %shard_map.137), channel_id=1, replica_groups=mesh['dp'=4,'context'=16,'tensor'=4] {'context'}, dimensions={0} | all-to-all | bytes 524288 | tf_op jit(solution)/shard_map/all_to_all | solution.py:418
  124.5 0.2 reshape.33
  124.7 0.3 copy.19
  125.1 0.3 reshape.34
  125.4 5.6 %convolution_convert_fusion = bf16[128,4096]{1,0:T(8,128)(2,1)} fusion(bf16[128,1024]{1,0:T(8,128)(2,1)S(1)} %reshape.34, bf16[1024,4096]{1,0:T(8,128)(2,1)} %param.27), kind=kOutput, calls=%fused_computation | convolution fusion | flops 1074266112 | bytes 9699328 | tf_op jit(solution)/shard_map/dot_general | solution.py:423
  131.0 0.0 reduce-scatter.2.cloned.1.call-update
  131.1 26.3 %reduce-scatter.2.cloned.1.call-done = bf16[32,4096]{1,0:T(8,128)(2,1)} async-done(((bf16[128,4096]{1,0:T(8,128)(2,1)}), bf16[32,4096]{1,0:T(8,128)(2,1)}) %reduce-scatter.2.cloned.1.call-update) | async-done | bytes 262160 | tf_op jit(solution)/shard_map/reduce_scatter | solution.py:422
  (3 shorter events, 0.0 us)
Async XLA Ops:
  6.5 150.9 %reduce-scatter.2.cloned.1.call-start = ((), (), s32[]{:S(2)}) async-start(), calls=%async_computation.2 | async-start | bytes 1310720 | tf_op jit(solution)/shard_map/reduce_scatter | solution.py:422
  7.3 1.0 copy-start
  8.3 0.9 copy-start.1
  9.2 0.9 copy-start.2
  10.2 0.9 copy-start.3
  11.1 0.7 copy-start.11
  45.2 0.7 copy-start.4
  45.9 0.7 copy-start.5
  46.6 0.7 copy-start.6
  47.3 0.7 copy-start.7
  47.9 0.7 copy-start.8
  48.6 0.7 copy-start.9
  49.3 0.7 copy-start.10
Sparse Core Ops, SparseCore 0:
  131.2 26.1 reduce-scatter.1
where the time goes:
time: 167 us; the launch traced here: 164 us
  Pallas kernels  94 us (56%)
  waiting for transfers between devices  26.3 us (16%)
  blocking collectives  13.8 us (8%)
  between operations  13.4 us (8%)
  local copies, waits for them, and re-layouts  10.9 us (7%)
  matrix products  5.62 us (3%)
    pallas_call x1, Pallas kernels, run_recur(): pl.pallas_call(functools.partial(recur, n_ctx, seq_len), out_shape=jax.Sh...  60.7 us
    pallas_call x1, Pallas kernels, local(): pl.pallas_call(functools.partial(exchange, n_ctx, n_peers, per_seq), out_...  33.4 us
    reduce_scatter x1, waiting for transfers between devices, local(): lax.psum_scatter(jnp.dot(lines, final_projection, preferred_element_type=...  26.3 us
    all_to_all x1, blocking collectives, local(): lax.all_to_all(normed, 'context', split_axis=0, concat_axis=0, tiled=True)  13.8 us
    unnamed x25, local copies, waits for them, and re-layouts  10 us
    dot_general x1, matrix products, local(): jnp.dot(lines, final_projection, preferred_element_type=f32).astype(bf16)  5.62 us
  transfers between devices with their start and end apart: 1, of which 1 were waited for; matrix products, arithmetic and copies ran while one was open for 0% of the time, Pallas kernels for 0%

commit v1 on v0

v1 whole, which is shorter than its diff:
```python
import functools

import jax
import jax.numpy as jnp
from jax import lax
from jax.experimental import pallas as pl
from jax.experimental.pallas import tpu as pltpu
from jax.sharding import PartitionSpec as P

MESH = pl.DeviceIdType.MESH
SPAN = 64
GROUP = 4
SMALL = 8
decay_cap = 0.606531
unit_eps = 1e-06
group_eps = 0.00064
f32 = jnp.float32
bf16 = jnp.bfloat16


def nn(a, b):
    return lax.dot_general(
        a.astype(bf16), b.astype(bf16), (((1,), (0,)), ((), ())), preferred_element_type=f32
    )


def nt(a, b):
    return lax.dot_general(
        a.astype(bf16), b.astype(bf16), (((1,), (1,)), ((), ())), preferred_element_type=f32
    )


def tn(a, b):
    return lax.dot_general(
        a.astype(bf16), b.astype(bf16), (((0,), (0,)), ((), ())), preferred_element_type=f32
    )


def exchange(
    n_ctx,
    n_peers,
    per_seq,
    r_ref,
    k_ref,
    v_ref,
    a_ref,
    code_ref,
    ptr_ref,
    rows_ref,
    meta_ref,
    packed,
    notes,
    send_sem,
    recv_sem,
    note_send,
    note_recv,
    own_sem,
):
    dp = lax.axis_index("dp")
    ctx = lax.axis_index("context")
    me = dp * n_ctx + ctx
    tensor = lax.axis_index("tensor")

    def place(index):
        return (index // n_ctx, lax.rem(index, n_ctx), tensor)

    barrier = pltpu.get_barrier_semaphore()

    def greet(step, carry):
        other = lax.rem(me + step, n_peers)
        pl.semaphore_signal(barrier, inc=1, device_id=place(other), device_id_type=MESH)
        return carry

    lax.fori_loop(1, n_peers, greet, 0)

    tokens = r_ref.shape[0]
    n_dp = n_peers // n_ctx
    for pair in range(n_ctx // 2):
        lanes = slice(128 * pair, 128 * pair + 128)
        left, right = slice(0, SPAN), slice(SPAN, 128)
        r, k, v, a = r_ref[:, lanes], k_ref[:, lanes], v_ref[:, lanes], a_ref[:, lanes]
        for half, part in ((0, left), (1, right)):
            rk = jnp.concatenate([r[:, part], k[:, part]], axis=1)
            va = jnp.concatenate([v[:, part], a[:, part]], axis=1)
            for s in range(n_dp):
                slot = s * n_ctx + 2 * pair + half
                packed[slot, :, 0:128] = rk[s * per_seq : (s + 1) * per_seq]
                packed[slot, :, 128:256] = va[s * per_seq : (s + 1) * per_seq]

    eye = (
        lax.broadcasted_iota(jnp.int32, (tokens, tokens), 0)
        == lax.broadcasted_iota(jnp.int32, (tokens, tokens), 1)
    ).astype(f32)
    codes = lax.dot_general(
        code_ref[...].astype(f32),
        eye,
        (((0,), (0,)), ((), ())),
        precision=lax.Precision.HIGHEST,
        preferred_element_type=f32,
    )
    pointers = ptr_ref[...].astype(f32)
    for c in range(n_ctx):
        notes[c, 0:1, :] = pointers
        notes[c, 1:2, :] = codes[c : c + 1, :]
        notes[c, 2:8, :] = jnp.zeros((6, tokens), f32)

    pl.semaphore_wait(barrier, n_peers - 1)

    own_rows = pltpu.make_async_copy(packed.at[me], rows_ref.at[me], own_sem.at[0])
    own_rows.start()
    own_note = pltpu.make_async_copy(notes.at[ctx], meta_ref.at[ctx], own_sem.at[1])
    own_note.start()

    def note_copy(step):
        other = lax.rem(ctx + step, n_ctx)
        return pltpu.make_async_remote_copy(
            src_ref=notes.at[other],
            dst_ref=meta_ref.at[ctx],
            send_sem=note_send,
            recv_sem=note_recv,
            device_id=(dp, other, tensor),
            device_id_type=MESH,
        )

    def rows_copy(step):
        other = lax.rem(me + step, n_peers)
        return pltpu.make_async_remote_copy(
            src_ref=packed.at[other],
            dst_ref=rows_ref.at[me],
            send_sem=send_sem,
            recv_sem=recv_sem,
            device_id=place(other),
            device_id_type=MESH,
        )

    def send_note(step, carry):
        note_copy(step).start()
        return carry

    def send_rows(step, carry):
        rows_copy(step).start()
        return carry

    lax.fori_loop(1, n_ctx, send_note, 0)
    lax.fori_loop(1, n_peers, send_rows, 0)
    own_rows.wait()
    own_note.wait()
    rest_rows = rows_ref.at[pl.ds(0, n_peers - 1)]
    rest_notes = meta_ref.at[pl.ds(0, n_ctx - 1)]
    pltpu.make_async_copy(rest_notes, rest_notes, note_send).wait()
    pltpu.make_async_copy(rest_notes, rest_notes, note_recv).wait()
    pltpu.make_async_copy(rest_rows, rest_rows, send_sem).wait()
    pltpu.make_async_copy(rest_rows, rest_rows, recv_sem).wait()


def recur(
    n_ctx,
    seq_len,
    rows_ref,
    meta_ref,
    lens_ref,
    rate_ref,
    gain_ref,
    mix_ref,
    bonus_ref,
    scale_ref,
    shift_ref,
    out_ref,
    wide_rk,
    wide_va,
):
    ctx = lax.axis_index("context")
    odd = lax.rem(ctx, 2) == 1
    n_src, per_seq = rows_ref.shape[0], rows_ref.shape[1]
    block = meta_ref.shape[2]
    lane = lax.broadcasted_iota(jnp.int32, (block, block), 1)
    row = lax.broadcasted_iota(jnp.int32, (block, block), 0)
    flip = (lane[:SPAN] & (SPAN - 1)) == row[:SPAN]

    lines = []
    for ref in (rate_ref, gain_ref, mix_ref, bonus_ref, scale_ref, shift_ref):
        lines.append(ref[pl.ds(ctx // 2, 1), :])
    lines = jnp.concatenate(lines + lines[:2], axis=0)
    lines = jnp.where(odd, lines[:, SPAN:], lines[:, :SPAN])

    def column(index):
        line = jnp.broadcast_to(lines[index : index + 1], (SPAN, SPAN))
        return jnp.sum(jnp.where(flip[:, :SPAN], line, 0.0), axis=1, keepdims=True) + jnp.zeros(
            (SPAN, block), f32
        )

    rate, gain, mix, bonus, scale, shift = [column(index) for index in range(6)]
    first = lens_ref[0, 0]
    second = first + lens_ref[0, 1]
    third = second + lens_ref[0, 2]

    def doc_start(position):
        found = jnp.where(position >= first, first, 0)
        found = jnp.where(position >= second, second, found)
        return jnp.where(position >= third, third, found)

    spread = rows_ref[...].reshape(n_src * per_seq, 4 * SPAN).astype(f32)
    wide_rk[...] = spread[:, : 2 * SPAN]
    wide_va[...] = spread[:, 2 * SPAN :]

    mid = block // 2
    sums = jnp.concatenate(
        [
            (row <= lane).astype(f32) - (row < mid).astype(f32),
            (row >= mid).astype(f32),
            (row < mid).astype(f32),
        ],
        axis=1,
    ).astype(bf16)
    eye = (row == lane).astype(f32)
    nbits = {}
    size = SMALL
    while size <= block:
        nbits[size] = (row // size) == (lane // size)
        size *= 2

    now = jnp.zeros((SPAN, SPAN), f32)
    for group in range(n_ctx // GROUP):
        ids = [group * GROUP + b for b in range(GROUP)]
        each = range(GROUP)
        got = []
        for c in ids:
            pointer = meta_ref[c, 0:1, :].astype(jnp.int32)
            where = (pointer & 1) * n_src + (pointer // 128)
            pick = (row == where).astype(bf16)
            parts = []
            for wide in (wide_rk, wide_va):
                even = wide[pl.ds(2 * c, n_src, stride=per_seq), :]
                uneven = wide[pl.ds(2 * c + 1, n_src, stride=per_seq), :]
                parts.append(jnp.concatenate([even, uneven], axis=0).T)
            got.append(nn(jnp.concatenate(parts, axis=0), pick))
        r = [g[:SPAN] for g in got]
        k = [g[SPAN : 2 * SPAN] for g in got]
        v = [g[2 * SPAN : 3 * SPAN] for g in got]
        a = [g[3 * SPAN :] for g in got]
        position = [c * block + lane[0:1] for c in ids]
        start = [doc_start(p) for p in position]
        start_last = [doc_start(c * block + block - 1) for c in ids]
        decay = [
            -decay_cap * (1.0 - jnp.exp(-rate * meta_ref[c, 1:2, :])) for c in ids
        ]
        cums = []
        for d in decay:
            d0 = d.astype(bf16)
            rest = d - d0.astype(f32)
            d1 = rest.astype(bf16)
            d2 = (rest - d1.astype(f32)).astype(bf16)
            total = nn(jnp.concatenate([d0, d1, d2], axis=0), sums)
            cums.append(total[:SPAN] + total[SPAN : 2 * SPAN] + total[2 * SPAN :])
        about = [x[:, :block] for x in cums]
        to_end = [x[:, block : 2 * block] for x in cums]
        to_mid = [x[:, 2 * block :] for x in cums]
        scaled = [x * gain for x in k]
        unit = [
            x * lax.rsqrt(jnp.sum(x * x, axis=0, keepdims=True) + unit_eps) for x in scaled
        ]
        mixed = [k[i] * (1.0 + (a[i] - 1.0) * mix) for i in each]
        erase = [jnp.where(start[i] == position[i], 0.0, unit[i] * a[i]) for i in each]
        extra = [
            jnp.sum(r[i] * mixed[i] * (bonus + 1.0), axis=0, keepdims=True) * v[i] for i in each
        ]
        down = [jnp.exp(-x) for x in about]
        unit_up = [unit[i] * jnp.exp(about[i] - decay[i]) for i in each]
        recept_up = [r[i] * jnp.exp(about[i]) for i in each]
        opening = [
            jnp.where(start[i] < ids[i] * block, jnp.exp(to_mid[i]), 0.0) for i in each
        ]
        unit_start = [unit_up[i] * opening[i] for i in each]
        recept_start = [recept_up[i] * opening[i] for i in each]
        erase_down = [(erase[i] * down[i]).T.astype(bf16) for i in each]
        mixed_down = [(mixed[i] * down[i]).T.astype(bf16) for i in each]
        ends = []
        for i in each:
            choice = jnp.where(lane[:SPAN] < SPAN, to_end[i], to_end[i] + to_mid[i])
            ends.append(jnp.exp(jnp.sum(jnp.where(flip, choice, 0.0), axis=0, keepdims=True)))
        fade = [x[:, :SPAN] for x in ends]
        keep = [
            jnp.where(start_last[i] < ids[i] * block, ends[i][:, SPAN:], 0.0) for i in each
        ]
        scores = [
            nn(
                jnp.concatenate([erase_down[i], mixed_down[i]], axis=0),
                jnp.concatenate([unit_up[i], recept_up[i]], axis=1),
            )
            for i in each
        ]
        inside = [row >= start[i] - ids[i] * block for i in each]
        strict = [inside[i] & (row < lane) for i in each]
        inclusive = [inside[i] & (row <= lane) for i in each]
        erase_mat = [jnp.where(strict[i], scores[i][:block, :block], 0.0) for i in each]
        read_erase = [
            jnp.where(inclusive[i], scores[i][:block, block:], 0.0).astype(bf16) for i in each
        ]
        write_mat = [
            jnp.where(strict[i], scores[i][block:, :block], 0.0).astype(bf16) for i in each
        ]
        read_write = [
            jnp.where(strict[i], scores[i][block:, block:], 0.0).astype(bf16) for i in each
        ]
        power = [jnp.where(nbits[SMALL], -x, 0.0) for x in erase_mat]
        inverse = [eye + x for x in power]
        size = 2
        while size < SMALL:
            power = [nn(x, x) for x in power]
            inverse = [inverse[i] + nn(inverse[i], power[i]) for i in each]
            size *= 2
        size = SMALL
        while size < block:
            ring = nbits[2 * size] & ~nbits[size]
            inner = [nn(jnp.where(ring, erase_mat[i], 0.0), inverse[i]) for i in each]
            inverse = [inverse[i] - nn(inverse[i], inner[i]) for i in each]
            size *= 2
        both = [
            nn(v[i], jnp.concatenate([write_mat[i], read_write[i]], axis=1)) for i in each
        ]
        solved = [
            nn(jnp.concatenate([both[i][:, :block], unit_start[i]], axis=0), inverse[i])
            for i in each
        ]
        read = [nn(solved[i], read_erase[i]) for i in each]
        local_out = [both[i][:, block:] - read[i][:SPAN] + extra[i] for i in each]
        carry_out = [(recept_start[i] - read[i][SPAN:]).astype(bf16) for i in each]
        last = [start[i] == start_last[i] for i in each]
        moved = [nn(jnp.where(last[i], solved[i], 0.0), erase_down[i]) for i in each]
        put = [nn(jnp.where(last[i], v[i], 0.0), mixed_down[i]) for i in each]
        push = [(put[i] - moved[i][:SPAN]) * fade[i] for i in each]
        trans = [(moved[i][SPAN:] * fade[i]).astype(bf16) for i in each]
        whole = []
        for i in each:
            carried = now.astype(bf16)
            whole.append(nn(carried, carry_out[i]) + local_out[i])
            now = now * keep[i] - nn(carried, trans[i]) + push[i]
        for i in each:
            center = whole[i] - jnp.mean(whole[i], axis=0, keepdims=True)
            power2 = jnp.mean(center * center, axis=0, keepdims=True)
            out_ref[ids[i]] = (center * lax.rsqrt(power2 + group_eps) * scale + shift).astype(bf16)


def vmem():
    return pl.BlockSpec(memory_space=pltpu.VMEM)


def run_recur(n_ctx, seq_len, block, rows, meta, lens, vectors):
    return pl.pallas_call(
        functools.partial(recur, n_ctx, seq_len),
        out_shape=jax.ShapeDtypeStruct((n_ctx, SPAN, block), bf16),
        in_specs=[vmem(), vmem(), pl.BlockSpec(memory_space=pltpu.SMEM)] + [vmem()] * 6,
        out_specs=vmem(),
        scratch_shapes=[
            pltpu.VMEM((seq_len, 2 * SPAN), f32),
            pltpu.VMEM((seq_len, 2 * SPAN), f32),
        ],
        compiler_params=pltpu.CompilerParams(vmem_limit_bytes=48 << 20),
    )(rows, meta, lens, *vectors)


def project(
    n_ctx,
    n_tensor,
    normed_ref,
    weight_ref,
    out_ref,
    weight,
    heads,
    parts,
    landed,
    load_sem,
    own_sem,
    head_send,
    head_recv,
    part_send,
    part_recv,
):
    dp = lax.axis_index("dp")
    ctx = lax.axis_index("context")
    tensor = lax.axis_index("tensor")
    barrier = pltpu.get_barrier_semaphore()
    n_parts, width = weight.shape[0], weight.shape[2]

    def load(n):
        return pltpu.make_async_copy(
            weight_ref.at[:, pl.ds(n * width, width)], weight.at[n], load_sem.at[n]
        )

    def greet(step, carry):
        other = lax.rem(ctx + step, n_ctx)
        pl.semaphore_signal(barrier, inc=1, device_id=(dp, other, tensor), device_id_type=MESH)
        return carry

    lax.fori_loop(1, n_ctx, greet, 0)
    for step in range(1, n_tensor):
        other = lax.rem(tensor + step, n_tensor)
        pl.semaphore_signal(barrier, inc=1, device_id=(dp, ctx, other), device_id_type=MESH)
    for n in range(n_parts):
        load(n).start()
    pl.semaphore_wait(barrier, n_ctx - 1 + n_tensor - 1)

    own = pltpu.make_async_copy(normed_ref.at[ctx], heads.at[ctx], own_sem)
    own.start()

    def send(step, carry):
        other = lax.rem(ctx + step, n_ctx)
        pltpu.make_async_remote_copy(
            src_ref=normed_ref.at[other],
            dst_ref=heads.at[ctx],
            send_sem=head_send,
            recv_sem=head_recv,
            device_id=(dp, other, tensor),
            device_id_type=MESH,
        ).start()
        return carry

    lax.fori_loop(1, n_ctx, send, 0)
    own.wait()
    rest = heads.at[pl.ds(0, n_ctx - 1)]
    pltpu.make_async_copy(rest, rest, head_recv).wait()
    lines = jnp.concatenate(
        [
            heads[2 * c : 2 * c + 2].reshape(2 * SPAN, heads.shape[2]).T
            for c in range(n_ctx // 2)
        ],
        axis=1,
    )

    def part_copy(n, step):
        other = lax.rem(tensor + step, n_tensor)
        return pltpu.make_async_remote_copy(
            src_ref=parts.at[n, other],
            dst_ref=landed.at[n, step - 1],
            send_sem=part_send.at[n, step - 1],
            recv_sem=part_recv.at[n, step - 1],
            device_id=(dp, ctx, other),
            device_id_type=MESH,
        )

    own_rows = parts.shape[2]
    for n in range(n_parts):
        load(n).wait()
        product = jnp.dot(lines, weight[n], preferred_element_type=f32).astype(bf16)
        for q in range(n_tensor):
            parts[n, q] = product[q * own_rows : (q + 1) * own_rows]
        for step in (2, 1, 3):
            part_copy(n, step).start()
    for n in range(n_parts):
        total = parts[n, tensor].astype(f32)
        for step in range(1, n_tensor):
            part_copy(n, step).wait_recv()
            total = total + landed[n, step - 1].astype(f32)
        out_ref[:, n * width : (n + 1) * width] = total.astype(bf16)
    pltpu.make_async_copy(rest, rest, head_send).wait()
    for n in range(n_parts):
        for step in range(1, n_tensor):
            part_copy(n, step).wait_send()


def run_project(n_ctx, n_tensor, tokens, normed, weight):
    depth, columns = weight.shape
    n_parts = 4
    own_rows = tokens // n_tensor
    width = columns // n_parts
    return pl.pallas_call(
        functools.partial(project, n_ctx, n_tensor),
        out_shape=jax.ShapeDtypeStruct((own_rows, columns), bf16),
        in_specs=[vmem(), pl.BlockSpec(memory_space=pl.ANY)],
        out_specs=vmem(),
        scratch_shapes=[
            pltpu.VMEM((n_parts, depth, width), bf16),
            pltpu.VMEM((n_ctx, SPAN, tokens), bf16),
            pltpu.VMEM((n_parts, n_tensor, own_rows, width), bf16),
            pltpu.VMEM((n_parts, n_tensor - 1, own_rows, width), bf16),
            pltpu.SemaphoreType.DMA((n_parts,)),
            pltpu.SemaphoreType.DMA,
            pltpu.SemaphoreType.DMA,
            pltpu.SemaphoreType.DMA,
            pltpu.SemaphoreType.DMA((n_parts, n_tensor - 1)),
            pltpu.SemaphoreType.DMA((n_parts, n_tensor - 1)),
        ],
        compiler_params=pltpu.CompilerParams(
            collective_id=1, has_side_effects=True, vmem_limit_bytes=48 << 20
        ),
    )(normed, weight)


def local(
    acceptance_vectors,
    lookup_vectors,
    payload_vectors,
    incontext_adaptation,
    fading_codes,
    stacked_line_pointer,
    article_extents,
    feature_fading,
    erasure_lookup_scaling,
    lookup_mixture_share,
    reward_coefficients,
    cluster_standard_scaling,
    cluster_standard_offset,
    final_projection,
):
    tokens, features = acceptance_vectors.shape
    n_dp = lax.axis_size("dp")
    n_ctx = lax.axis_size("context")
    n_peers = n_dp * n_ctx
    per_seq = tokens // n_dp
    seq_len = tokens * n_ctx
    rows, meta = pl.pallas_call(
        functools.partial(exchange, n_ctx, n_peers, per_seq),
        out_shape=(
            jax.ShapeDtypeStruct((n_peers, per_seq, 4 * SPAN), bf16),
            jax.ShapeDtypeStruct((n_ctx, 8, tokens), f32),
        ),
        in_specs=[vmem()] * 6,
        out_specs=(vmem(), vmem()),
        scratch_shapes=[
            pltpu.VMEM((n_peers, per_seq, 4 * SPAN), bf16),
            pltpu.VMEM((n_ctx, 8, tokens), f32),
            pltpu.SemaphoreType.DMA,
            pltpu.SemaphoreType.DMA,
            pltpu.SemaphoreType.DMA,
            pltpu.SemaphoreType.DMA,
            pltpu.SemaphoreType.DMA((2,)),
        ],
        compiler_params=pltpu.CompilerParams(
            collective_id=0, has_side_effects=True, vmem_limit_bytes=32 << 20
        ),
    )(
        acceptance_vectors,
        lookup_vectors,
        payload_vectors,
        incontext_adaptation,
        fading_codes[0],
        stacked_line_pointer,
    )
    vectors = [
        item.reshape(features // 128, 128)
        for item in (
            feature_fading,
            erasure_lookup_scaling,
            lookup_mixture_share,
            reward_coefficients,
            cluster_standard_scaling,
            cluster_standard_offset,
        )
    ]
    normed = run_recur(n_ctx, seq_len, tokens, rows, meta, article_extents, vectors)
    n_tensor = lax.axis_size("tensor")
    summed = run_project(n_ctx, n_tensor, tokens, normed, final_projection)
    return summed.reshape(1, tokens // n_tensor, final_projection.shape[1])


def solution(mesh):
    return jax.shard_map(
        local,
        mesh=mesh,
        in_specs=(
            P(("dp", "context"), "tensor"),
            P(("dp", "context"), "tensor"),
            P(("dp", "context"), "tensor"),
            P(("dp", "context"), "tensor"),
            P("dp", "context", "tensor"),
            P("dp", "context"),
            P("dp", None),
            P("tensor"),
            P("tensor"),
            P("tensor"),
            P("tensor"),
            P("tensor"),
            P("tensor"),
            P("tensor", None),
        ),
        out_specs=P("dp", ("context", "tensor"), None),
        check_vma=False,
    )
```

time: 167 us -> 91 us (0.54)
  the two profiles are of different devices: /device:TPU:192 before, /device:TPU:1 now
where the time goes in v1:
time: 91 us; the launch traced here: 90.5 us
  Pallas kernels  79.8 us (88%)
  local copies, waits for them, and re-layouts  10.7 us (12%)
    pallas_call x1, Pallas kernels, local(): pl.pallas_call(functools.partial(exchange, n_ctx, n_peers, per_seq), out_...  36.6 us
    pallas_call x1, Pallas kernels, run_project(): pl.pallas_call(functools.partial(project, n_ctx, n_tensor), out_shape=jax...  28.5 us
    pallas_call x1, Pallas kernels, run_recur(): pl.pallas_call(functools.partial(recur, n_ctx, seq_len), out_shape=jax.Sh...  14.7 us
    unnamed x26, local copies, waits for them, and re-layouts  10.7 us

profile of v1, /device:TPU:1, one launch (start us, length us, event | category | flops | bytes accessed | tf_op | source)
XLA Modules:
  0.0 90.5 jit_solution(16121757114510975696)
XLA Ops:
  0.0 0.8 copy.15
  0.8 0.0 copy-start
  0.8 0.9 %copy-done = bf16[128,1024]{1,0:T(8,128)(2,1)S(1)} copy-done((bf16[128,1024]{1,0:T(8,128)(2,1)S(1)}, bf16[128,1024]{1,0:T(8,128)(2,1)}, u32[]{:S(2)}) %copy-start) | copy-done | bytes 262168
  1.7 0.0 copy-start.1
  1.8 0.9 %copy-done.1 = bf16[128,1024]{1,0:T(8,128)(2,1)S(1)} copy-done((bf16[128,1024]{1,0:T(8,128)(2,1)S(1)}, bf16[128,1024]{1,0:T(8,128)(2,1)}, u32[]{:S(2)}) %copy-start.1) | copy-done | bytes 262168
  2.7 0.0 copy-start.2
  2.7 0.9 %copy-done.2 = bf16[128,1024]{1,0:T(8,128)(2,1)S(1)} copy-done((bf16[128,1024]{1,0:T(8,128)(2,1)S(1)}, bf16[128,1024]{1,0:T(8,128)(2,1)}, u32[]{:S(2)}) %copy-start.2) | copy-done | bytes 262168
  3.6 0.0 copy-start.3
  3.7 0.9 %copy-done.3 = bf16[128,1024]{1,0:T(8,128)(2,1)S(1)} copy-done((bf16[128,1024]{1,0:T(8,128)(2,1)S(1)}, bf16[128,1024]{1,0:T(8,128)(2,1)}, u32[]{:S(2)}) %copy-start.3) | copy-done | bytes 262168
  4.6 0.0 copy-start.11
  4.6 0.7 copy-done.11
  5.3 36.6 %shard_map.136 = (bf16[64,32,256]{2,1,0:T(8,128)(2,1)S(1)}, f32[16,8,128]{2,1,0:T(8,128)S(1)}) custom-call(bf16[128,1024]{1,0:T(8,128)(2,1)S(1)} %copy-done, bf16[128,1024]{1,0:T(8,128)(2,1)S(1)} %copy-done.1, bf16[128,1024]{1,0:T(8,128)(2,1)S(1)} %copy-done.2, bf16[128,1024]{1,0:T(8,128)(2,1)S(1)} %copy-done.3, s32[128,16]{1,0:T(8,128)S(1)} %bitcast.9, ...), custom_call_target="tpu_custom_call" | custom-call | tf_op jit(solution)/shard_map/pallas_call | solution.py:511
  41.9 0.0 copy-start.4
  41.9 0.7 copy-done.4
  42.6 0.0 copy-start.5
  42.6 0.7 copy-done.5
  43.3 0.0 copy-start.6
  43.3 0.7 copy-done.6
  44.0 0.0 copy-start.7
  44.0 0.7 copy-done.7
  44.6 0.0 copy-start.8
  44.6 0.7 copy-done.8
  45.3 0.0 copy-start.9
  45.3 0.7 copy-done.9
  46.0 0.0 copy-start.10
  46.0 0.7 copy-done.10
  46.7 14.7 %shard_map.137.normed_ref = bf16[16,64,128]{2,1,0:T(8,128)(2,1)S(1)} custom-call(bf16[64,32,256]{2,1,0:T(8,128)(2,1)S(1)} %get-tuple-element.7.rows_ref, f32[16,8,128]{2,1,0:T(8,128)S(1)} %get-tuple-element.8.meta_ref, s32[1,4]{1,0:T(1,128)S(1)} %copy-done.10, f32[8,128]{1,0:T(8,128)S(1)} %bitcast.10, f32[8,128]{1,0:T(8,128)S(1)} %bitcast.11, ...), custom_call_target="tpu_custom_call" | custom-call | tf_op jit(solution)/shard_map/pallas_call | solution.py:349
  61.3 28.5 %shard_map.138 = bf16[32,4096]{1,0:T(8,128)(2,1)S(1)} custom-call(bf16[16,64,128]{2,1,0:T(8,128)(2,1)S(1)} %shard_map.137.normed_ref, bf16[1024,4096]{1,0:T(8,128)(2,1)} %weight_ref.1), custom_call_target="tpu_custom_call" | custom-call | tf_op jit(solution)/shard_map/pallas_call | solution.py:466
  89.8 0.7 copy.17
Async XLA Ops:
  0.8 1.0 %copy-start = (bf16[128,1024]{1,0:T(8,128)(2,1)S(1)}, bf16[128,1024]{1,0:T(8,128)(2,1)}, u32[]{:S(2)}) copy-start(bf16[128,1024]{1,0:T(8,128)(2,1)} %r_ref.1) | copy-start | bytes 786436
  1.7 0.9 %copy-start.1 = (bf16[128,1024]{1,0:T(8,128)(2,1)S(1)}, bf16[128,1024]{1,0:T(8,128)(2,1)}, u32[]{:S(2)}) copy-start(bf16[128,1024]{1,0:T(8,128)(2,1)} %k_ref.1) | copy-start | bytes 786436
  2.7 0.9 %copy-start.2 = (bf16[128,1024]{1,0:T(8,128)(2,1)S(1)}, bf16[128,1024]{1,0:T(8,128)(2,1)}, u32[]{:S(2)}) copy-start(bf16[128,1024]{1,0:T(8,128)(2,1)} %v_ref.1) | copy-start | bytes 786436
  3.6 0.9 %copy-start.3 = (bf16[128,1024]{1,0:T(8,128)(2,1)S(1)}, bf16[128,1024]{1,0:T(8,128)(2,1)}, u32[]{:S(2)}) copy-start(bf16[128,1024]{1,0:T(8,128)(2,1)} %a_ref.1) | copy-start | bytes 786436
  4.6 0.7 copy-start.11
  41.9 0.7 copy-start.4
  42.6 0.7 copy-start.5
  43.3 0.7 copy-start.6
  44.0 0.7 copy-start.7
  44.6 0.7 copy-start.8
  45.3 0.7 copy-start.9
  46.0 0.7 copy-start.10

commit v2 on v1

v2 whole, which is shorter than its diff:
```python
import functools

import jax
import jax.numpy as jnp
from jax import lax
from jax.experimental import pallas as pl
from jax.experimental.pallas import tpu as pltpu
from jax.sharding import PartitionSpec as P

MESH = pl.DeviceIdType.MESH
SPAN = 64
GROUP = 4
SMALL = 8
PARTS = 4
decay_cap = 0.606531
unit_eps = 1e-06
group_eps = 0.00064
f32 = jnp.float32
bf16 = jnp.bfloat16


def nn(a, b):
    return lax.dot_general(
        a.astype(bf16), b.astype(bf16), (((1,), (0,)), ((), ())), preferred_element_type=f32
    )


def layer(
    n_dp,
    n_ctx,
    n_tensor,
    r_hbm,
    k_hbm,
    v_hbm,
    a_hbm,
    code_hbm,
    ptr_hbm,
    lens_hbm,
    rate_hbm,
    gain_hbm,
    mix_hbm,
    bonus_hbm,
    scale_hbm,
    shift_hbm,
    weight_hbm,
    out_ref,
    r_ref,
    k_ref,
    v_ref,
    a_ref,
    code_ref,
    ptr_ref,
    lens_ref,
    lines_ref,
    weight,
    packed,
    rows,
    wide,
    notes,
    meta,
    pre,
    tips,
    picks,
    normed,
    heads,
    parts,
    landed,
    load_sem,
    weight_sem,
    own_sem,
    note_send,
    note_recv,
    rows_send,
    rows_recv,
    head_send,
    head_recv,
    part_send,
    part_recv,
):
    dp = lax.axis_index("dp")
    ctx = lax.axis_index("context")
    tensor = lax.axis_index("tensor")
    n_peers = n_dp * n_ctx
    me = dp * n_ctx + ctx
    block = r_ref.shape[0]
    n_groups = n_ctx // GROUP
    width = weight.shape[2]

    loads = [
        (r_hbm, r_ref),
        (k_hbm, k_ref),
        (v_hbm, v_ref),
        (a_hbm, a_ref),
        (code_hbm, code_ref),
        (ptr_hbm, ptr_ref),
        (lens_hbm, lens_ref),
    ]
    for i, ref in enumerate((rate_hbm, gain_hbm, mix_hbm, bonus_hbm, scale_hbm, shift_hbm)):
        loads.append((ref, lines_ref.at[i]))
    loads = [
        pltpu.make_async_copy(src, dst, load_sem.at[i]) for i, (src, dst) in enumerate(loads)
    ]
    for load in loads:
        load.start()

    def place(index):
        return (index // n_ctx, lax.rem(index, n_ctx), tensor)

    barrier = pltpu.get_barrier_semaphore()

    def greet(step, carry):
        other = lax.rem(me + step, n_peers)
        pl.semaphore_signal(barrier, inc=1, device_id=place(other), device_id_type=MESH)
        return carry

    lax.fori_loop(1, n_peers, greet, 0)
    for step in range(1, n_tensor):
        other = lax.rem(tensor + step, n_tensor)
        pl.semaphore_signal(barrier, inc=1, device_id=(dp, ctx, other), device_id_type=MESH)

    def weight_load(n):
        return pltpu.make_async_copy(
            weight_hbm.at[:, pl.ds(n * width, width)], weight.at[n], weight_sem.at[n]
        )

    for load in loads:
        load.wait()
    for n in range(PARTS):
        weight_load(n).start()

    per_seq = block // n_dp
    for pair in range(n_ctx // 2):
        lanes = slice(128 * pair, 128 * pair + 128)
        r, k, v, a = r_ref[:, lanes], k_ref[:, lanes], v_ref[:, lanes], a_ref[:, lanes]
        for half, part in ((0, slice(0, SPAN)), (1, slice(SPAN, 128))):
            rk = jnp.concatenate([r[:, part], k[:, part]], axis=1).astype(f32)
            va = jnp.concatenate([v[:, part], a[:, part]], axis=1).astype(f32)
            for s in range(n_dp):
                slot = s * n_ctx + 2 * pair + half
                for g in range(n_groups):
                    piece = slice(s * per_seq + 8 * g, s * per_seq + 8 * g + 8)
                    packed[g, slot] = jnp.concatenate([rk[piece], va[piece]], axis=0).astype(bf16)
    codes = code_ref[...].astype(f32)
    pointers = ptr_ref[...].astype(f32)
    for c in range(n_ctx):
        notes[c] = jnp.concatenate(
            [pointers, codes[c : c + 1, :], jnp.zeros((6, block), f32)], axis=0
        )

    pl.semaphore_wait(barrier, n_peers - 1 + n_tensor - 1)

    own = [pltpu.make_async_copy(notes.at[ctx], meta.at[ctx], own_sem.at[n_groups])]
    for g in range(n_groups):
        own.append(pltpu.make_async_copy(packed.at[g, me], rows.at[g, me], own_sem.at[g]))
    for copy in own:
        copy.start()

    def send_note(step, carry):
        other = lax.rem(ctx + step, n_ctx)
        pltpu.make_async_remote_copy(
            src_ref=notes.at[other],
            dst_ref=meta.at[ctx],
            send_sem=note_send,
            recv_sem=note_recv,
            device_id=(dp, other, tensor),
            device_id_type=MESH,
        ).start()
        return carry

    lax.fori_loop(1, n_ctx, send_note, 0)
    for g in range(n_groups):

        def send_rows(step, carry, g=g):
            other = lax.rem(me + step, n_peers)
            pltpu.make_async_remote_copy(
                src_ref=packed.at[g, other],
                dst_ref=rows.at[g, me],
                send_sem=rows_send.at[g],
                recv_sem=rows_recv.at[g],
                device_id=place(other),
                device_id_type=MESH,
            ).start()
            return carry

        lax.fori_loop(1, n_peers, send_rows, 0)

    odd = lax.rem(ctx, 2) == 1
    lane = lax.broadcasted_iota(jnp.int32, (block, block), 1)
    row = lax.broadcasted_iota(jnp.int32, (block, block), 0)
    flip = (lane[:SPAN] & (SPAN - 1)) == row[:SPAN]

    def column(index):
        line = lines_ref[index, pl.ds(ctx // 2, 1), :]
        line = jnp.where(odd, line[:, SPAN:], line[:, :SPAN])
        line = jnp.broadcast_to(line, (SPAN, SPAN))
        return jnp.sum(jnp.where(flip[:, :SPAN], line, 0.0), axis=1, keepdims=True) + jnp.zeros(
            (SPAN, block), f32
        )

    rate, gain, mix, bonus, scale, shift = [column(index) for index in range(6)]
    lens = lens_ref[...]
    first = lens[:, 0:1]
    second = first + lens[:, 1:2]
    third = second + lens[:, 2:3]

    def doc_start(position):
        found = jnp.where(position >= first, first, 0)
        found = jnp.where(position >= second, second, found)
        return jnp.where(position >= third, third, found)

    mid = block // 2
    sums = jnp.concatenate(
        [
            (row <= lane).astype(f32) - (row < mid).astype(f32),
            (row >= mid).astype(f32),
            (row < mid).astype(f32),
        ],
        axis=1,
    ).astype(bf16)
    eye = (row == lane).astype(f32)
    nbits = {}
    size = SMALL
    while size <= block:
        nbits[size] = (row // size) == (lane // size)
        size *= 2
    own[0].wait()
    rest = meta.at[pl.ds(0, n_ctx - 1)]
    pltpu.make_async_copy(rest, rest, note_recv).wait()
    each = range(GROUP)
    for group in range(n_groups):
        ids = [group * GROUP + b for b in each]
        decay = [-decay_cap * (1.0 - jnp.exp(-rate * meta[c, 1:2, :])) for c in ids]
        cums = []
        for d in decay:
            d0 = d.astype(bf16)
            left = d - d0.astype(f32)
            d1 = left.astype(bf16)
            d2 = (left - d1.astype(f32)).astype(bf16)
            total = nn(jnp.concatenate([d0, d1, d2], axis=0), sums)
            cums.append(total[:SPAN] + total[SPAN : 2 * SPAN] + total[2 * SPAN :])
        for i, c in enumerate(ids):
            position = c * block + lane[0:1]
            start = doc_start(position)
            about = cums[i][:, :block]
            to_end = cums[i][:, block : 2 * block]
            to_mid = cums[i][:, 2 * block :]
            pre[c, 0] = jnp.exp(about)
            pre[c, 1] = jnp.exp(-about)
            pre[c, 2] = jnp.exp(about - decay[i])
            pre[c, 3] = jnp.where(start < c * block, jnp.exp(to_mid), 0.0)
            choice = jnp.where(lane[:SPAN] < SPAN, to_end, to_end + to_mid)
            ends = jnp.exp(jnp.sum(jnp.where(flip, choice, 0.0), axis=0, keepdims=True))
            through = doc_start(c * block + block - 1 + jnp.zeros((1, block), jnp.int32)) < c * block
            ends = jnp.where(through | (lane[0:1] < SPAN), ends, 0.0)
            tips[c] = jnp.broadcast_to(ends, (8, block))
            pointer = meta[c, 0:1, :].astype(jnp.int32)
            where = (pointer & 1) * n_peers + (pointer // block)
            picks[c] = (row == where).astype(bf16)

    def head_copy(c):
        return pltpu.make_async_remote_copy(
            src_ref=normed.at[c],
            dst_ref=heads.at[ctx],
            send_sem=head_send,
            recv_sem=head_recv,
            device_id=(dp, c, tensor),
            device_id_type=MESH,
        )

    now = jnp.zeros((SPAN, SPAN), f32)
    for group in range(n_groups):
        ids = [group * GROUP + b for b in each]
        own[1 + group].wait()
        rest = rows.at[group, pl.ds(0, n_peers - 1)]
        pltpu.make_async_copy(rest, rest, rows_recv.at[group]).wait()
        wide[...] = rows[group].reshape(n_peers * 16, 2 * SPAN).astype(f32)
        got = []
        for c in ids:
            kinds = []
            for offset in (2 * (c % GROUP), 2 * (c % GROUP) + 8):
                even = wide[pl.ds(offset, n_peers, stride=16), :]
                uneven = wide[pl.ds(offset + 1, n_peers, stride=16), :]
                kinds.append(jnp.concatenate([even, uneven], axis=0).T)
            got.append(nn(jnp.concatenate(kinds, axis=0), picks[c]))
        r = [g[:SPAN] for g in got]
        k = [g[SPAN : 2 * SPAN] for g in got]
        v = [g[2 * SPAN : 3 * SPAN] for g in got]
        a = [g[3 * SPAN :] for g in got]
        position = [c * block + lane[0:1] for c in ids]
        start = [doc_start(p) for p in position]
        zeros = jnp.zeros((1, block), jnp.int32)
        start_last = [doc_start(c * block + block - 1 + zeros) for c in ids]
        scaled = [x * gain for x in k]
        unit = [
            x * lax.rsqrt(jnp.sum(x * x, axis=0, keepdims=True) + unit_eps) for x in scaled
        ]
        mixed = [k[i] * (1.0 + (a[i] - 1.0) * mix) for i in each]
        erase = [jnp.where(start[i] == position[i], 0.0, unit[i] * a[i]) for i in each]
        extra = [
            jnp.sum(r[i] * mixed[i] * (bonus + 1.0), axis=0, keepdims=True) * v[i] for i in each
        ]
        recept_up = [r[i] * pre[ids[i], 0] for i in each]
        down = [pre[c, 1] for c in ids]
        unit_up = [unit[i] * pre[ids[i], 2] for i in each]
        opening = [pre[c, 3] for c in ids]
        unit_start = [unit_up[i] * opening[i] for i in each]
        recept_start = [recept_up[i] * opening[i] for i in each]
        erase_down = [(erase[i] * down[i]).T.astype(bf16) for i in each]
        mixed_down = [(mixed[i] * down[i]).T.astype(bf16) for i in each]
        fade = [tips[c, 0:1, :SPAN] for c in ids]
        keep = [tips[c, 0:1, SPAN:] for c in ids]
        scores = [
            nn(
                jnp.concatenate([erase_down[i], mixed_down[i]], axis=0),
                jnp.concatenate([unit_up[i], recept_up[i]], axis=1),
            )
            for i in each
        ]
        inside = [row >= start[i] - ids[i] * block for i in each]
        strict = [inside[i] & (row < lane) for i in each]
        inclusive = [inside[i] & (row <= lane) for i in each]
        erase_mat = [jnp.where(strict[i], scores[i][:block, :block], 0.0) for i in each]
        read_erase = [
            jnp.where(inclusive[i], scores[i][:block, block:], 0.0).astype(bf16) for i in each
        ]
        write_mat = [
            jnp.where(strict[i], scores[i][block:, :block], 0.0).astype(bf16) for i in each
        ]
        read_write = [
            jnp.where(strict[i], scores[i][block:, block:], 0.0).astype(bf16) for i in each
        ]
        power = [jnp.where(nbits[SMALL], -x, 0.0) for x in erase_mat]
        inverse = [eye + x for x in power]
        size = 2
        while size < SMALL:
            power = [nn(x, x) for x in power]
            inverse = [inverse[i] + nn(inverse[i], power[i]) for i in each]
            size *= 2
        size = SMALL
        while size < block:
            ring = nbits[2 * size] & ~nbits[size]
            inner = [nn(jnp.where(ring, erase_mat[i], 0.0), inverse[i]) for i in each]
            inverse = [inverse[i] - nn(inverse[i], inner[i]) for i in each]
            size *= 2
        both = [
            nn(v[i], jnp.concatenate([write_mat[i], read_write[i]], axis=1)) for i in each
        ]
        solved = [
            nn(jnp.concatenate([both[i][:, :block], unit_start[i]], axis=0), inverse[i])
            for i in each
        ]
        read = [nn(solved[i], read_erase[i]) for i in each]
        local_out = [both[i][:, block:] - read[i][:SPAN] + extra[i] for i in each]
        carry_out = [(recept_start[i] - read[i][SPAN:]).astype(bf16) for i in each]
        last = [start[i] == start_last[i] for i in each]
        moved = [nn(jnp.where(last[i], solved[i], 0.0), erase_down[i]) for i in each]
        put = [nn(jnp.where(last[i], v[i], 0.0), mixed_down[i]) for i in each]
        push = [(put[i] - moved[i][:SPAN]) * fade[i] for i in each]
        trans = [(moved[i][SPAN:] * fade[i]).astype(bf16) for i in each]
        whole = []
        for i in each:
            carried = now.astype(bf16)
            whole.append(nn(carried, carry_out[i]) + local_out[i])
            now = now * keep[i] - nn(carried, trans[i]) + push[i]
        for i in each:
            center = whole[i] - jnp.mean(whole[i], axis=0, keepdims=True)
            power2 = jnp.mean(center * center, axis=0, keepdims=True)
            line = (center * lax.rsqrt(power2 + group_eps) * scale + shift).astype(bf16)
            normed[ids[i]] = line

            @pl.when(ctx == ids[i])
            def _(i=i, line=line):
                heads[ids[i]] = line

            @pl.when(ctx != ids[i])
            def _(i=i):
                head_copy(ids[i]).start()

    rest_heads = heads.at[pl.ds(0, n_ctx - 1)]
    pltpu.make_async_copy(rest_heads, rest_heads, head_recv).wait()
    lines = jnp.concatenate(
        [heads[2 * c : 2 * c + 2].reshape(2 * SPAN, block).T for c in range(n_ctx // 2)], axis=1
    )

    def part_copy(n, step):
        other = lax.rem(tensor + step, n_tensor)
        return pltpu.make_async_remote_copy(
            src_ref=parts.at[n, other],
            dst_ref=landed.at[n, step - 1],
            send_sem=part_send.at[n, step - 1],
            recv_sem=part_recv.at[n, step - 1],
            device_id=(dp, ctx, other),
            device_id_type=MESH,
        )

    own_rows = parts.shape[2]
    for n in range(PARTS):
        weight_load(n).wait()
        product = jnp.dot(lines, weight[n], preferred_element_type=f32).astype(bf16)
        for q in range(n_tensor):
            parts[n, q] = product[q * own_rows : (q + 1) * own_rows]
        for step in (2, 1, 3):
            part_copy(n, step).start()
    for n in range(PARTS):
        total = parts[n, tensor].astype(f32)
        for step in range(1, n_tensor):
            part_copy(n, step).wait_recv()
            total = total + landed[n, step - 1].astype(f32)
        out_ref[:, n * width : (n + 1) * width] = total.astype(bf16)
    rest = meta.at[pl.ds(0, n_ctx - 1)]
    pltpu.make_async_copy(rest, rest, note_send).wait()
    for g in range(n_groups):
        rest = rows.at[g, pl.ds(0, n_peers - 1)]
        pltpu.make_async_copy(rest, rest, rows_send.at[g]).wait()
    pltpu.make_async_copy(rest_heads, rest_heads, head_send).wait()
    for n in range(PARTS):
        for step in range(1, n_tensor):
            part_copy(n, step).wait_send()


def hbm():
    return pl.BlockSpec(memory_space=pltpu.HBM)


def local(
    acceptance_vectors,
    lookup_vectors,
    payload_vectors,
    incontext_adaptation,
    fading_codes,
    stacked_line_pointer,
    article_extents,
    feature_fading,
    erasure_lookup_scaling,
    lookup_mixture_share,
    reward_coefficients,
    cluster_standard_scaling,
    cluster_standard_offset,
    final_projection,
):
    tokens, features = acceptance_vectors.shape
    columns = final_projection.shape[1]
    n_dp = lax.axis_size("dp")
    n_ctx = lax.axis_size("context")
    n_tensor = lax.axis_size("tensor")
    n_peers = n_dp * n_ctx
    n_groups = n_ctx // GROUP
    own_rows = tokens // n_tensor
    width = columns // PARTS
    vectors = [
        item.reshape(features // 128, 128)
        for item in (
            feature_fading,
            erasure_lookup_scaling,
            lookup_mixture_share,
            reward_coefficients,
            cluster_standard_scaling,
            cluster_standard_offset,
        )
    ]
    dma = pltpu.SemaphoreType.DMA
    vm = pltpu.VMEM
    summed = pl.pallas_call(
        functools.partial(layer, n_dp, n_ctx, n_tensor),
        out_shape=jax.ShapeDtypeStruct((own_rows, columns), bf16),
        in_specs=[hbm()] * 14,
        out_specs=pl.BlockSpec(memory_space=pltpu.VMEM),
        scratch_shapes=[
            vm((tokens, features), bf16),
            vm((tokens, features), bf16),
            vm((tokens, features), bf16),
            vm((tokens, features), bf16),
            vm((n_ctx, tokens), jnp.int32),
            vm((1, tokens), jnp.int32),
            vm((1, article_extents.shape[1]), jnp.int32),
            vm((6, features // 128, 128), f32),
            vm((PARTS, features, width), bf16),
            vm((n_groups, n_peers, 16, 2 * SPAN), bf16),
            vm((n_groups, n_peers, 16, 2 * SPAN), bf16),
            vm((n_peers * 16, 2 * SPAN), f32),
            vm((n_ctx, 8, tokens), f32),
            vm((n_ctx, 8, tokens), f32),
            vm((n_ctx, 4, SPAN, tokens), f32),
            vm((n_ctx, 8, tokens), f32),
            vm((n_ctx, tokens, tokens), bf16),
            vm((n_ctx, SPAN, tokens), bf16),
            vm((n_ctx, SPAN, tokens), bf16),
            vm((PARTS, n_tensor, own_rows, width), bf16),
            vm((PARTS, n_tensor - 1, own_rows, width), bf16),
            dma((13,)),
            dma((PARTS,)),
            dma((n_groups + 1,)),
            dma,
            dma,
            dma((n_groups,)),
            dma((n_groups,)),
            dma,
            dma,
            dma((PARTS, n_tensor - 1)),
            dma((PARTS, n_tensor - 1)),
        ],
        compiler_params=pltpu.CompilerParams(
            collective_id=0, has_side_effects=True, vmem_limit_bytes=52 << 20
        ),
    )(
        acceptance_vectors,
        lookup_vectors,
        payload_vectors,
        incontext_adaptation,
        fading_codes[0].T,
        stacked_line_pointer,
        article_extents,
        *vectors,
        final_projection,
    )
    return summed.reshape(1, own_rows, columns)


def solution(mesh):
    return jax.shard_map(
        local,
        mesh=mesh,
        in_specs=(
            P(("dp", "context"), "tensor"),
            P(("dp", "context"), "tensor"),
            P(("dp", "context"), "tensor"),
            P(("dp", "context"), "tensor"),
            P("dp", "context", "tensor"),
            P("dp", "context"),
            P("dp", None),
            P("tensor"),
            P("tensor"),
            P("tensor"),
            P("tensor"),
            P("tensor"),
            P("tensor"),
            P("tensor", None),
        ),
        out_specs=P("dp", ("context", "tensor"), None),
        check_vma=False,
    )
```

time: 91 us -> 71.8 us (0.79)
  the two profiles are of different devices: /device:TPU:1 before, /device:TPU:192 now
where the time goes in v2:
time: 71.8 us; the launch traced here: 71.4 us
  Pallas kernels  60.7 us (85%)
  local copies, waits for them, and re-layouts  10.6 us (15%)
    pallas_call x1, Pallas kernels, local(): pl.pallas_call(functools.partial(layer, n_dp, n_ctx, n_tensor), out_shape...  60.7 us
    unnamed x27, local copies, waits for them, and re-layouts  10.6 us

profile of v2, /device:TPU:192, one launch (start us, length us, event | category | flops | bytes accessed | tf_op | source)
XLA Modules:
  0.0 71.4 jit_solution(12207539286596536626)
XLA Ops:
  0.0 0.0 copy-start
  0.0 0.9 %copy-done = bf16[128,1024]{1,0:T(8,128)(2,1)S(1)} copy-done((bf16[128,1024]{1,0:T(8,128)(2,1)S(1)}, bf16[128,1024]{1,0:T(8,128)(2,1)}, u32[]{:S(2)}) %copy-start) | copy-done | bytes 262168
  1.0 0.0 copy-start.1
  1.0 0.9 %copy-done.1 = bf16[128,1024]{1,0:T(8,128)(2,1)S(1)} copy-done((bf16[128,1024]{1,0:T(8,128)(2,1)S(1)}, bf16[128,1024]{1,0:T(8,128)(2,1)}, u32[]{:S(2)}) %copy-start.1) | copy-done | bytes 262168
  1.9 0.0 copy-start.2
  1.9 0.9 %copy-done.2 = bf16[128,1024]{1,0:T(8,128)(2,1)S(1)} copy-done((bf16[128,1024]{1,0:T(8,128)(2,1)S(1)}, bf16[128,1024]{1,0:T(8,128)(2,1)}, u32[]{:S(2)}) %copy-start.2) | copy-done | bytes 262168
  2.9 0.0 copy-start.3
  2.9 0.9 %copy-done.3 = bf16[128,1024]{1,0:T(8,128)(2,1)S(1)} copy-done((bf16[128,1024]{1,0:T(8,128)(2,1)S(1)}, bf16[128,1024]{1,0:T(8,128)(2,1)}, u32[]{:S(2)}) %copy-start.3) | copy-done | bytes 262168
  3.8 0.0 copy-start.4
  3.8 0.7 copy-done.4
  4.5 0.0 copy-start.5
  4.5 0.7 copy-done.5
  5.2 0.0 copy-start.6
  5.2 0.7 copy-done.6
  5.9 0.0 copy-start.7
  5.9 0.7 copy-done.7
  6.6 0.0 copy-start.8
  6.6 0.7 copy-done.8
  7.2 0.0 copy-start.9
  7.3 0.7 copy-done.9
  7.9 0.0 copy-start.10
  7.9 0.7 copy-done.10
  8.6 0.0 copy-start.11
  8.6 0.7 copy-done.11
  9.3 0.0 copy-start.12
  9.3 0.7 copy-done.12
  9.9 60.7 %shard_map.136 = bf16[32,4096]{1,0:T(8,128)(2,1)S(1)} custom-call(bf16[128,1024]{1,0:T(8,128)(2,1)S(1)} %copy-done, bf16[128,1024]{1,0:T(8,128)(2,1)S(1)} %copy-done.1, bf16[128,1024]{1,0:T(8,128)(2,1)S(1)} %copy-done.2, bf16[128,1024]{1,0:T(8,128)(2,1)S(1)} %copy-done.3, s32[16,128]{1,0:T(8,128)S(1)} %bitcast.11, s32[1,128]{1,0:T(1,128)S(1)} %copy-done.11, ...), custom_call_target="tpu_custom_call" | custom-call | tf_op jit(solution)/shard_map/pallas_call | solution.py:463
  70.7 0.7 copy.16
Async XLA Ops:
  0.0 0.9 %copy-start = (bf16[128,1024]{1,0:T(8,128)(2,1)S(1)}, bf16[128,1024]{1,0:T(8,128)(2,1)}, u32[]{:S(2)}) copy-start(bf16[128,1024]{1,0:T(8,128)(2,1)} %r_hbm.1) | copy-start | bytes 786436
  1.0 0.9 %copy-start.1 = (bf16[128,1024]{1,0:T(8,128)(2,1)S(1)}, bf16[128,1024]{1,0:T(8,128)(2,1)}, u32[]{:S(2)}) copy-start(bf16[128,1024]{1,0:T(8,128)(2,1)} %k_hbm.1) | copy-start | bytes 786436
  1.9 0.9 %copy-start.2 = (bf16[128,1024]{1,0:T(8,128)(2,1)S(1)}, bf16[128,1024]{1,0:T(8,128)(2,1)}, u32[]{:S(2)}) copy-start(bf16[128,1024]{1,0:T(8,128)(2,1)} %v_hbm.1) | copy-start | bytes 786436
  2.9 0.9 %copy-start.3 = (bf16[128,1024]{1,0:T(8,128)(2,1)S(1)}, bf16[128,1024]{1,0:T(8,128)(2,1)}, u32[]{:S(2)}) copy-start(bf16[128,1024]{1,0:T(8,128)(2,1)} %a_hbm.1) | copy-start | bytes 786436
  3.8 0.7 copy-start.4
  4.5 0.7 copy-start.5
  5.2 0.7 copy-start.6
  5.9 0.7 copy-start.7
  6.6 0.7 copy-start.8
  7.2 0.7 copy-start.9
  7.9 0.7 copy-start.10
  8.6 0.7 copy-start.11
  9.3 0.7 copy-start.12

commit v3 on v2

--- a/solution.py
+++ b/solution.py
@@ -86,6 +86,21 @@
     n_groups = n_ctx // GROUP
     width = weight.shape[2]
 
+    def place(index):
+        return (index // n_ctx, lax.rem(index, n_ctx), tensor)
+
+    barrier = pltpu.get_barrier_semaphore()
+
+    def greet(step, carry):
+        other = lax.rem(me + step, n_peers)
+        pl.semaphore_signal(barrier, inc=1, device_id=place(other), device_id_type=MESH)
+        return carry
+
+    lax.fori_loop(1, n_peers, greet, 0)
+    for step in range(1, n_tensor):
+        other = lax.rem(tensor + step, n_tensor)
+        pl.semaphore_signal(barrier, inc=1, device_id=(dp, ctx, other), device_id_type=MESH)
+
     loads = [
         (r_hbm, r_ref),
         (k_hbm, k_ref),
@@ -102,21 +117,6 @@
     ]
     for load in loads:
         load.start()
-
-    def place(index):
-        return (index // n_ctx, lax.rem(index, n_ctx), tensor)
-
-    barrier = pltpu.get_barrier_semaphore()
-
-    def greet(step, carry):
-        other = lax.rem(me + step, n_peers)
-        pl.semaphore_signal(barrier, inc=1, device_id=place(other), device_id_type=MESH)
-        return carry
-
-    lax.fori_loop(1, n_peers, greet, 0)
-    for step in range(1, n_tensor):
-        other = lax.rem(tensor + step, n_tensor)
-        pl.semaphore_signal(barrier, inc=1, device_id=(dp, ctx, other), device_id_type=MESH)
 
     def weight_load(n):
         return pltpu.make_async_copy(
@@ -500,7 +500,7 @@
             dma((PARTS, n_tensor - 1)),
         ],
         compiler_params=pltpu.CompilerParams(
-            collective_id=0, has_side_effects=True, vmem_limit_bytes=52 << 20
+            collective_id=0, has_side_effects=True, vmem_limit_bytes=60 << 20
         ),
     )(
         acceptance_vectors,

time: 71.8 us -> 63 us (0.88)
  local copies, waits for them, and re-layouts: 10.6 us -> 1.67 us
    unnamed x27 -> x1, local copies, waits for them, and re-layouts: 10.6 us -> 1.67 us
where the time goes in v3:
time: 63 us; the launch traced here: 62.9 us
  Pallas kernels  61.2 us (97%)
  local copies, waits for them, and re-layouts  1.67 us (3%)
    pallas_call x1, Pallas kernels, local(): pl.pallas_call(functools.partial(layer, n_dp, n_ctx, n_tensor), out_shape...  61.2 us
    unnamed x1, local copies, waits for them, and re-layouts  1.67 us

profile of v3, /device:TPU:192, one launch (start us, length us, event | category | flops | bytes accessed | tf_op | source)
XLA Modules:
  0.0 62.9 jit_solution(3932953843194448558)
XLA Ops:
  0.0 61.2 %shard_map.136 = bf16[32,4096]{1,0:T(8,128)(2,1)} custom-call(bf16[128,1024]{1,0:T(8,128)(2,1)} %r_hbm.1, bf16[128,1024]{1,0:T(8,128)(2,1)} %k_hbm.1, bf16[128,1024]{1,0:T(8,128)(2,1)} %v_hbm.1, bf16[128,1024]{1,0:T(8,128)(2,1)} %a_hbm.1, s32[16,128]{1,0:T(8,128)} %bitcast.11, s32[1,128]{1,0:T(1,128)} %ptr_hbm.1, s32[1,4]{1,0:T(1,128)} %lens_hbm.1, ...), custom_call_target="tpu_custom_call" | custom-call | tf_op jit(solution)/shard_map/pallas_call | solution.py:463
  61.2 1.7 %copy.16 = bf16[1,32,4096]{2,1,0:T(8,128)(2,1)} copy(bf16[1,32,4096]{2,1,0:T(8,128)(2,1)} %bitcast.10) | data formatting | bytes 524288

commit v4 on v3

--- a/solution.py
+++ b/solution.py
@@ -11,7 +11,8 @@
 SPAN = 64
 GROUP = 4
 SMALL = 8
-PARTS = 4
+PARTS = 8
+LAG = 6
 decay_cap = 0.606531
 unit_eps = 1e-06
 group_eps = 0.00064
@@ -64,6 +65,8 @@
     normed,
     heads,
     parts,
+    relay_in,
+    relay_out,
     landed,
     load_sem,
     weight_sem,
@@ -382,16 +385,36 @@
         [heads[2 * c : 2 * c + 2].reshape(2 * SPAN, block).T for c in range(n_ctx // 2)], axis=1
     )
 
-    def part_copy(n, step):
-        other = lax.rem(tensor + step, n_tensor)
+    def toward(n, far):
+        step = n_tensor - 1 if (n % 2 == 0) != far else 1
+        return lax.rem(tensor + step, n_tensor)
+
+    def copy_to(n, kind, src, dst, other):
         return pltpu.make_async_remote_copy(
-            src_ref=parts.at[n, other],
-            dst_ref=landed.at[n, step - 1],
-            send_sem=part_send.at[n, step - 1],
-            recv_sem=part_recv.at[n, step - 1],
+            src_ref=src,
+            dst_ref=dst,
+            send_sem=part_send.at[n, kind],
+            recv_sem=part_recv.at[n, kind],
             device_id=(dp, ctx, other),
             device_id_type=MESH,
         )
+
+    def raw_copy(n):
+        opposite = lax.rem(tensor + 2, n_tensor)
+        return copy_to(n, 0, parts.at[n, opposite], relay_in.at[n], toward(n, False))
+
+    def straight_copy(n):
+        other = toward(n, True)
+        return copy_to(n, 1, parts.at[n, other], landed.at[n, 0], other)
+
+    def sum_copy(n):
+        return copy_to(n, 2, relay_out.at[n], landed.at[n, 1], toward(n, False))
+
+    def relay(n):
+        raw_copy(n).wait_recv()
+        both = relay_in[n].astype(f32) + parts[n, toward(n, False)].astype(f32)
+        relay_out[n] = both.astype(bf16)
+        sum_copy(n).start()
 
     own_rows = parts.shape[2]
     for n in range(PARTS):
@@ -399,13 +422,16 @@
         product = jnp.dot(lines, weight[n], preferred_element_type=f32).astype(bf16)
         for q in range(n_tensor):
             parts[n, q] = product[q * own_rows : (q + 1) * own_rows]
-        for step in (2, 1, 3):
-            part_copy(n, step).start()
+        raw_copy(n).start()
+        straight_copy(n).start()
+        if n >= LAG:
+            relay(n - LAG)
+    for n in range(PARTS - LAG, PARTS):
+        relay(n)
     for n in range(PARTS):
-        total = parts[n, tensor].astype(f32)
-        for step in range(1, n_tensor):
-            part_copy(n, step).wait_recv()
-            total = total + landed[n, step - 1].astype(f32)
+        straight_copy(n).wait_recv()
+        sum_copy(n).wait_recv()
+        total = parts[n, tensor].astype(f32) + landed[n, 0].astype(f32) + landed[n, 1].astype(f32)
         out_ref[:, n * width : (n + 1) * width] = total.astype(bf16)
     rest = meta.at[pl.ds(0, n_ctx - 1)]
     pltpu.make_async_copy(rest, rest, note_send).wait()
@@ -414,8 +440,9 @@
         pltpu.make_async_copy(rest, rest, rows_send.at[g]).wait()
     pltpu.make_async_copy(rest_heads, rest_heads, head_send).wait()
     for n in range(PARTS):
-        for step in range(1, n_tensor):
-            part_copy(n, step).wait_send()
+        raw_copy(n).wait_send()
+        straight_copy(n).wait_send()
+        sum_copy(n).wait_send()
 
 
 def hbm():
@@ -486,7 +513,9 @@
             vm((n_ctx, SPAN, tokens), bf16),
             vm((n_ctx, SPAN, tokens), bf16),
             vm((PARTS, n_tensor, own_rows, width), bf16),
-            vm((PARTS, n_tensor - 1, own_rows, width), bf16),
+            vm((PARTS, own_rows, width), bf16),
+            vm((PARTS, own_rows, width), bf16),
+            vm((PARTS, 2, own_rows, width), bf16),
             dma((13,)),
             dma((PARTS,)),
             dma((n_groups + 1,)),
@@ -496,8 +525,8 @@
             dma((n_groups,)),
             dma,
             dma,
-            dma((PARTS, n_tensor - 1)),
-            dma((PARTS, n_tensor - 1)),
+            dma((PARTS, 3)),
+            dma((PARTS, 3)),
         ],
         compiler_params=pltpu.CompilerParams(
             collective_id=0, has_side_effects=True, vmem_limit_bytes=60 << 20

time: 63 us -> 60.6 us (0.962)
  Pallas kernels: 61.2 us -> 58.8 us
    pallas_call x1, Pallas kernels: 61.2 us -> 58.8 us  [local(): pl.pallas_call(functools.partial(layer, n_dp, n_ctx, n_tensor), out_shape...]
where the time goes in v4:
time: 60.6 us; the launch traced here: 60.5 us
  Pallas kernels  58.8 us (97%)
  local copies, waits for them, and re-layouts  1.67 us (3%)
    pallas_call x1, Pallas kernels, local(): pl.pallas_call(functools.partial(layer, n_dp, n_ctx, n_tensor), out_shape...  58.8 us
    unnamed x1, local copies, waits for them, and re-layouts  1.67 us

profile of v4, /device:TPU:192, one launch (start us, length us, event | category | flops | bytes accessed | tf_op | source)
XLA Modules:
  0.0 60.5 jit_solution(17647433215246513024)
XLA Ops:
  0.0 58.8 %shard_map.136 = bf16[32,4096]{1,0:T(8,128)(2,1)} custom-call(bf16[128,1024]{1,0:T(8,128)(2,1)} %r_hbm.1, bf16[128,1024]{1,0:T(8,128)(2,1)} %k_hbm.1, bf16[128,1024]{1,0:T(8,128)(2,1)} %v_hbm.1, bf16[128,1024]{1,0:T(8,128)(2,1)} %a_hbm.1, s32[16,128]{1,0:T(8,128)} %bitcast.11, s32[1,128]{1,0:T(1,128)} %ptr_hbm.1, s32[1,4]{1,0:T(1,128)} %lens_hbm.1, ...), custom_call_target="tpu_custom_call" | custom-call | tf_op jit(solution)/shard_map/pallas_call | solution.py:490
  58.8 1.7 %copy.16 = bf16[1,32,4096]{2,1,0:T(8,128)(2,1)} copy(bf16[1,32,4096]{2,1,0:T(8,128)(2,1)} %bitcast.10) | data formatting | bytes 524288

commit v5 on v4

--- a/solution.py
+++ b/solution.py
@@ -146,9 +146,7 @@
     codes = code_ref[...].astype(f32)
     pointers = ptr_ref[...].astype(f32)
     for c in range(n_ctx):
-        notes[c] = jnp.concatenate(
-            [pointers, codes[c : c + 1, :], jnp.zeros((6, block), f32)], axis=0
-        )
+        notes[c] = jnp.concatenate([pointers, codes[c : c + 1, :]], axis=0)
 
     pl.semaphore_wait(barrier, n_peers - 1 + n_tensor - 1)
 
@@ -505,8 +503,8 @@
             vm((n_groups, n_peers, 16, 2 * SPAN), bf16),
             vm((n_groups, n_peers, 16, 2 * SPAN), bf16),
             vm((n_peers * 16, 2 * SPAN), f32),
-            vm((n_ctx, 8, tokens), f32),
-            vm((n_ctx, 8, tokens), f32),
+            vm((n_ctx, 2, tokens), f32),
+            vm((n_ctx, 2, tokens), f32),
             vm((n_ctx, 4, SPAN, tokens), f32),
             vm((n_ctx, 8, tokens), f32),
             vm((n_ctx, tokens, tokens), bf16),

time: 60.6 us -> 59.6 us (0.983)
  Pallas kernels: 58.8 us -> 57.8 us
    pallas_call x1, Pallas kernels: 58.8 us -> 57.8 us  [local(): pl.pallas_call(functools.partial(layer, n_dp, n_ctx, n_tensor), out_shape...]
where the time goes in v5:
time: 59.6 us; the launch traced here: 59.5 us
  Pallas kernels  57.8 us (97%)
  local copies, waits for them, and re-layouts  1.67 us (3%)
    pallas_call x1, Pallas kernels, local(): pl.pallas_call(functools.partial(layer, n_dp, n_ctx, n_tensor), out_shape...  57.8 us
    unnamed x1, local copies, waits for them, and re-layouts  1.67 us

profile of v5, /device:TPU:192, one launch (start us, length us, event | category | flops | bytes accessed | tf_op | source)
XLA Modules:
  0.0 59.5 jit_solution(7753090810552975802)
XLA Ops:
  0.0 57.8 %shard_map.136 = bf16[32,4096]{1,0:T(8,128)(2,1)} custom-call(bf16[128,1024]{1,0:T(8,128)(2,1)} %r_hbm.1, bf16[128,1024]{1,0:T(8,128)(2,1)} %k_hbm.1, bf16[128,1024]{1,0:T(8,128)(2,1)} %v_hbm.1, bf16[128,1024]{1,0:T(8,128)(2,1)} %a_hbm.1, s32[16,128]{1,0:T(8,128)} %bitcast.11, s32[1,128]{1,0:T(1,128)} %ptr_hbm.1, s32[1,4]{1,0:T(1,128)} %lens_hbm.1, ...), custom_call_target="tpu_custom_call" | custom-call | tf_op jit(solution)/shard_map/pallas_call | solution.py:488
  57.8 1.7 %copy.16 = bf16[1,32,4096]{2,1,0:T(8,128)(2,1)} copy(bf16[1,32,4096]{2,1,0:T(8,128)(2,1)} %bitcast.10) | data formatting | bytes 524288

commit v6 on v5

--- a/solution.py
+++ b/solution.py
@@ -99,7 +99,8 @@
         pl.semaphore_signal(barrier, inc=1, device_id=place(other), device_id_type=MESH)
         return carry
 
-    lax.fori_loop(1, n_peers, greet, 0)
+    for step in range(1, n_peers):
+        greet(step, 0)
     for step in range(1, n_tensor):
         other = lax.rem(tensor + step, n_tensor)
         pl.semaphore_signal(barrier, inc=1, device_id=(dp, ctx, other), device_id_type=MESH)
@@ -128,8 +129,6 @@
 
     for load in loads:
         load.wait()
-    for n in range(PARTS):
-        weight_load(n).start()
 
     per_seq = block // n_dp
     for pair in range(n_ctx // 2):
@@ -184,6 +183,9 @@
             return carry
 
         lax.fori_loop(1, n_peers, send_rows, 0)
+
+    for n in range(PARTS):
+        weight_load(n).start()
 
     odd = lax.rem(ctx, 2) == 1
     lane = lax.broadcasted_iota(jnp.int32, (block, block), 1)
@@ -363,7 +365,6 @@
             carried = now.astype(bf16)
             whole.append(nn(carried, carry_out[i]) + local_out[i])
             now = now * keep[i] - nn(carried, trans[i]) + push[i]
-        for i in each:
             center = whole[i] - jnp.mean(whole[i], axis=0, keepdims=True)
             power2 = jnp.mean(center * center, axis=0, keepdims=True)
             line = (center * lax.rsqrt(power2 + group_eps) * scale + shift).astype(bf16)

time: 59.6 us -> 58.7 us (0.985)
  Pallas kernels: 57.8 us -> 56.8 us
    pallas_call x1, Pallas kernels: 57.8 us -> 56.8 us  [local(): pl.pallas_call(functools.partial(layer, n_dp, n_ctx, n_tensor), out_shape...]
where the time goes in v6:
time: 58.7 us; the launch traced here: 58.5 us
  Pallas kernels  56.8 us (97%)
  local copies, waits for them, and re-layouts  1.67 us (3%)
    pallas_call x1, Pallas kernels, local(): pl.pallas_call(functools.partial(layer, n_dp, n_ctx, n_tensor), out_shape...  56.8 us
    unnamed x1, local copies, waits for them, and re-layouts  1.67 us

profile of v6, /device:TPU:192, one launch (start us, length us, event | category | flops | bytes accessed | tf_op | source)
XLA Modules:
  0.0 58.5 jit_solution(10821264631029114678)
XLA Ops:
  0.0 56.8 %shard_map.136 = bf16[32,4096]{1,0:T(8,128)(2,1)} custom-call(bf16[128,1024]{1,0:T(8,128)(2,1)} %r_hbm.1, bf16[128,1024]{1,0:T(8,128)(2,1)} %k_hbm.1, bf16[128,1024]{1,0:T(8,128)(2,1)} %v_hbm.1, bf16[128,1024]{1,0:T(8,128)(2,1)} %a_hbm.1, s32[16,128]{1,0:T(8,128)} %bitcast.11, s32[1,128]{1,0:T(1,128)} %ptr_hbm.1, s32[1,4]{1,0:T(1,128)} %lens_hbm.1, ...), custom_call_target="tpu_custom_call" | custom-call | tf_op jit(solution)/shard_map/pallas_call | solution.py:489
  56.8 1.7 %copy.16 = bf16[1,32,4096]{2,1,0:T(8,128)(2,1)} copy(bf16[1,32,4096]{2,1,0:T(8,128)(2,1)} %bitcast.10) | data formatting | bytes 524288
